TPU v7x, 256 devices: a whole 4x4x8 slice. The times are simulated.
256 devices in a mesh: tm: 32 (over z_lo, x, core), op: 8 (over y, z_hi).
Axes of the slice: x: 4, y: 4, z: 8 (z_hi: 2, z_lo: 4; z = z_hi * 4 + z_lo), core: 2. Of those that a mesh axis runs over, the one named last changes fastest.
Arguments:
- peram: bfloat16 [32, 2, 256, 256], P('tm'), may hold values from -0.375 to 0.375
- sink_elementals: bfloat16 [32, 96, 2, 256, 256], P('tm', 'op'), may hold values from -0.375 to 0.375
- source_elementals: bfloat16 [96, 2, 256, 256], P('tm', None, 'op'), may hold values from -0.375 to 0.375
- irrep: int32 [96], replicated, may hold values from 0 to 3
Outputs:
- corr: float32 [32, 2, 96, 96], P('tm', None, 'op')
All inputs are finite; a program needn't handle non-finite values.
Results may differ from a plain program's by a relative error of at most 0.0041.
Values may be sent and summed in bfloat16 or wider, within the bound.
A program may use at most 128 MiB of HBM per device.

v0:
```python
import jax
import jax.numpy as jnp
from jax import lax
from jax.sharding import PartitionSpec as P


def pair_traces(turn_re, turn_im, src_re, src_im):
    full_re = jnp.einsum(
        "toba,jba->toj", turn_re, src_re, preferred_element_type=jnp.float32
    ) - jnp.einsum("toba,jba->toj", turn_im, src_im, preferred_element_type=jnp.float32)
    complete_imaginary = jnp.einsum(
        "toba,jba->toj", turn_re, src_im, preferred_element_type=jnp.float32
    ) + jnp.einsum("toba,jba->toj", turn_im, src_re, preferred_element_type=jnp.float32)
    return jnp.stack([full_re, complete_imaginary], axis=1)


def local(peram, sink_elementals, source_elementals, irrep):
    width = peram.shape[-1]
    quarter = width // 4
    slice_index = jnp.arange(width)
    signs = jnp.where(slice_index < 2 * quarter, 1.0, -1.0).astype(jnp.float32)
    both = (signs[:, None] * signs[None, :]).astype(jnp.bfloat16)
    tau_re = peram[:, 0]
    tau_im = peram[:, 1]
    bar_re = tau_re * both[None]
    barred_imaginary = -(tau_im * both[None])
    el_re = sink_elementals[:, :, 0]
    el_im = sink_elementals[:, :, 1]
    prod_re = jnp.einsum(
        "tocd,tde->toce", el_re, tau_re, preferred_element_type=jnp.float32
    ) - jnp.einsum("tocd,tde->toce", el_im, tau_im, preferred_element_type=jnp.float32)
    prod_im = jnp.einsum(
        "tocd,tde->toce", el_re, tau_im, preferred_element_type=jnp.float32
    ) + jnp.einsum("tocd,tde->toce", el_im, tau_re, preferred_element_type=jnp.float32)
    prod_re = prod_re.astype(jnp.bfloat16)
    prod_im = prod_im.astype(jnp.bfloat16)
    turn_re = jnp.einsum(
        "tocb,tca->toba", prod_re, bar_re, preferred_element_type=jnp.float32
    ) - jnp.einsum("tocb,tca->toba", prod_im, barred_imaginary, preferred_element_type=jnp.float32)
    turn_im = jnp.einsum(
        "tocb,tca->toba", prod_re, barred_imaginary, preferred_element_type=jnp.float32
    ) + jnp.einsum("tocb,tca->toba", prod_im, bar_re, preferred_element_type=jnp.float32)
    turn_re = turn_re.astype(jnp.bfloat16)
    turn_im = turn_im.astype(jnp.bfloat16)
    group_ops = sink_elementals.shape[1]
    rows = lax.all_gather(source_elementals, "op", axis=2, tiled=True)
    whole = lax.all_gather(rows, "tm", axis=0, tiled=True)
    mine = pair_traces(turn_re, turn_im, whole[:, 0], whole[:, 1])
    first = lax.axis_index("op") * group_ops
    own_labels = lax.dynamic_slice_in_dim(irrep, first, group_ops, 0)
    same = (own_labels[:, None] == irrep[None, :]).astype(jnp.float32)
    return mine * same[None, None, :, :]


def solution(mesh):
    return jax.shard_map(
        local,
        mesh=mesh,
        in_specs=(
            P("tm", None, None, None),
            P("tm", "op", None, None, None),
            P("tm", None, "op", None),
            P(),
        ),
        out_specs=P("tm", None, "op", None),
        check_vma=False,
    )
```

profile of v0, /device:TPU:1, one launch (start us, length us, event | category | flops | bytes accessed | tf_op | source)
XLA Modules:
  0.0 297.6 jit_solution(3388592611698042429)
XLA Ops:
  6.5 1.1 copy.21
  7.7 56.7 %all_gather.6 = bf16[3,2,256,256]{3,1,0,2:T(2,128)(2,1)S(1)} all-gather(bf16[3,2,32,256]{3,1,0,2:T(2,128)(2,1)S(1)} %copy.21), channel_id=1, replica_groups=mesh['tm'=32,'op'=8] {'op'}, dimensions={2}, use_global_device_ids=true | all-gather | bytes 884736 | tf_op jit(solution)/shard_map/all_gather | solution.py:46
  64.4 1.0 copy.22
  65.5 0.6 fusion.10
  66.0 0.6 fusion.12
  66.6 0.6 subtract_convert_fusion.1
  67.2 0.7 fusion.58
  67.9 0.6 add_convert_fusion.1
  68.5 1.1 copy-done.2
  69.6 1.9 add_convert_fusion
  71.5 3.5 %copy.28 = bf16[12,256,256]{1,0,2:T(8,128)(2,1)S(1)} copy(bf16[12,256,256]{2,1,0:T(8,128)(2,1)} %add_convert_fusion) | data formatting | bytes 3145728 | tf_op jit(solution)/shard_map/convert_element_type | solution.py:44
  75.0 2.2 fusion.56
  77.2 1.9 subtract_convert_fusion
  79.1 4.5 %copy.24 = bf16[12,256,256]{1,0,2:T(8,128)(2,1)} copy(bf16[12,256,256]{2,1,0:T(8,128)(2,1)} %subtract_convert_fusion) | data formatting | bytes 3145728 | tf_op jit(solution)/shard_map/convert_element_type | solution.py:43
  83.8 127.3 %all-gather.2.cloned.1.call-done = bf16[96,2,256,256]{3,2,1,0:T(8,128)(2,1)} async-done(((bf16[3,2,256,256]{3,2,1,0:T(8,128)(2,1)}), bf16[96,2,256,256]{3,2,1,0:T(8,128)(2,1)}) %all-gather.2.cloned.1.call-update) | async-done | bytes 25165840 | tf_op jit(solution)/shard_map/all_gather | solution.py:47
  211.1 17.4 %fusion.61 = (bf16[96,1,256,256]{3,2,1,0:T(8,128)(2,1)}, bf16[96,1,256,256]{3,2,1,0:T(8,128)(2,1)}) fusion(bf16[96,2,256,256]{3,2,1,0:T(8,128)(2,1)} %all-gather.2.cloned.1.call-done), kind=kLoop, calls=%fused_computation.49 | loop fusion | bytes 50331648 | tf_op jit(solution)/shard_map/slice | solution.py:48
  228.5 16.9 %copy.39 = bf16[96,1,256,256]{2,0,3,1:T(8,128)(2,1)} copy(bf16[96,1,256,256]{3,2,1,0:T(8,128)(2,1)} %get-tuple-element.5) | data formatting | bytes 25165824
  245.4 16.6 %copy.38 = bf16[96,1,256,256]{2,0,3,1:T(8,128)(2,1)} copy(bf16[96,1,256,256]{3,2,1,0:T(8,128)(2,1)} %get-tuple-element.6) | data formatting | bytes 25165824
  262.0 6.5 %fusion.21 = f32[12,96]{1,0:T(8,128)S(1)} fusion(bf16[12,256,256]{1,0,2:T(8,128)(2,1)S(1)} %copy.28, bf16[96,1,256,256]{2,0,3,1:T(8,128)(2,1)} %copy.38), kind=kOutput, calls=%fused_computation.23 | convolution fusion | flops 150994944 | bytes 14160384 | tf_op jit(solution)/shard_map/toba,jba->toj/dot_general | solution.py:13
  268.5 1.7 copy-done
  270.2 4.9 %fusion.18 = f32[12,96]{1,0:T(8,128)S(1)} fusion(bf16[12,256,256]{1,0,2:T(8,128)(2,1)} %copy.24, bf16[96,1,256,256]{2,0,3,1:T(8,128)(2,1)S(1)} %copy-done), kind=kOutput, calls=%fused_computation.22 | convolution fusion | flops 150994944 | bytes 14160384 | tf_op jit(solution)/shard_map/toba,jba->toj/dot_general | solution.py:8
  275.1 8.6 %fusion.33 = f32[1,1,12,96]{3,2,1,0:T(8,128)S(1)} fusion(f32[12,96]{1,0:T(8,128)S(1)} %fusion.21, bf16[12,256,256]{1,0,2:T(8,128)(2,1)} %copy.24, bf16[96,1,256,256]{2,0,3,1:T(8,128)(2,1)} %copy.39), kind=kOutput, calls=%fused_computation.27 | convolution fusion | flops 150996096 | bytes 14164992 | tf_op jit(solution)/shard_map/toba,jba->toj/dot_general | solution.py:11
  283.7 6.3 %fusion.39 = f32[1,1,12,96]{3,2,1,0:T(8,128)S(1)} fusion(f32[12,96]{1,0:T(8,128)S(1)} %fusion.18, bf16[12,256,256]{1,0,2:T(8,128)(2,1)S(1)} %copy.28, bf16[96,1,256,256]{2,0,3,1:T(8,128)(2,1)} %copy.39), kind=kOutput, calls=%fused_computation.29 | convolution fusion | flops 150996096 | bytes 14164992 | tf_op jit(solution)/shard_map/toba,jba->toj/dot_general | solution.py:10
  290.1 0.6 copy.31
  (18 shorter events, 0.2 us)
Async XLA Ops:
  6.5 58.9 %copy-start.5 = (bf16[1,2,256,256]{3,2,1,0:T(8,128)(2,1)S(1)}, bf16[1,2,256,256]{3,2,1,0:T(8,128)(2,1)}, u32[]{:S(2)}) copy-start(bf16[1,2,256,256]{3,2,1,0:T(8,128)(2,1)} %param.4) | copy-start | bytes 786436
  6.5 58.9 %copy-start.4 = (bf16[1,12,2,256,256]{4,3,2,1,0:T(8,128)(2,1)S(1)}, bf16[1,12,2,256,256]{4,3,2,1,0:T(8,128)(2,1)}, u32[]{:S(2)}) copy-start(bf16[1,12,2,256,256]{4,3,2,1,0:T(8,128)(2,1)} %param.5) | copy-start | bytes 9437188
  6.5 204.6 %all-gather.2.cloned.1.call-start = ((), (), s32[]{:S(2)}) async-start(), calls=%async_computation | async-start | bytes 25952256 | tf_op jit(solution)/shard_map/all_gather | solution.py:47
  67.2 1.3 copy-start.1
  68.5 1.1 copy-start.2
  75.0 2.2 copy-start.3
  79.1 4.5 %copy-start.6 = (s32[96]{0:T(128)S(1)}, s32[96]{0:T(128)}, u32[]{:S(2)}) copy-start(s32[96]{0:T(128)} %param.7) | copy-start | bytes 1156
  262.0 8.2 %copy-start = (bf16[96,1,256,256]{2,0,3,1:T(8,128)(2,1)S(1)}, bf16[96,1,256,256]{2,0,3,1:T(8,128)(2,1)}, u32[]{:S(2)}) copy-start(bf16[96,1,256,256]{2,0,3,1:T(8,128)(2,1)} %copy.38) | copy-start | bytes 37748740
Sparse Core Ops, SparseCore 0:
  65.5 145.5 all-gather.1
where the time goes:
time: 299 us; the launch traced here: 298 us
  waiting for transfers between devices  127 us (42%)
  local copies, waits for them, and re-layouts  64.6 us (22%)
  blocking collectives  56.7 us (19%)
  matrix products  35.3 us (12%)
  between operations  13.5 us (5%)
    all_gather x1, waiting for transfers between devices, local(): whole = lax.all_gather(rows, 'tm', axis=0, tiled=True)  127 us
    all_gather x1, blocking collectives, local(): rows = lax.all_gather(source_elementals, 'op', axis=2, tiled=True)  56.7 us
    unnamed x17, local copies, waits for them, and re-layouts  37.6 us
    slice x1, local copies, waits for them, and re-layouts, local(): mine = pair_traces(turn_re, turn_im, whole[:, 0], whole[:, 1])  17.4 us
    dot_general x1, matrix products, pair_traces(): jnp.einsum('toba,jba->toj', turn_re, src_im, preferred_element_type=jnp.f...  8.61 us
    dot_general x1, matrix products, pair_traces(): jnp.einsum('toba,jba->toj', turn_im, src_re, preferred_element_type=jnp.f...  6.46 us
    dot_general x1, matrix products, pair_traces(): jnp.einsum('toba,jba->toj', turn_im, src_im, preferred_element_type=jnp.f...  6.34 us
  transfers between devices with their start and end apart: 1, of which 1 were waited for; matrix products, arithmetic and copies ran while one was open for 6% of the time, Pallas kernels for 0%

commit v1 on v0

v1 whole, which is shorter than its diff:
```python
import jax
import jax.numpy as jnp
from jax import lax
from jax.experimental import pallas as pl
from jax.experimental.pallas import tpu as pltpu
from jax.sharding import PartitionSpec as P

MESH = pl.DeviceIdType.MESH
BF = jnp.bfloat16
F32 = jnp.float32
GROUPS = 3
STRIDE_T = 128
STRIDE_S = 48

HOPS = (
    ((0, 0), (0, 0)),
    ((1, 0), (1, 0)),
    ((3, 0), (3, 0)),
    ((0, 1), (0, 1)),
    ((0, 3), (0, 3)),
    ((3, 3), (3, 3)),
    ((1, 3), (3, 1)),
    ((2, 0), (0, 2)),
)


def dot_t(a, b):
    return lax.dot_general(a, b, (((1,), (1,)), ((), ())), preferred_element_type=F32)


def kernel(
    peram_ref, sink_ref, src_ref, out_ref,
    per_v, sink_v, src_v, left, bar, tout, recv, sring, fs, ft, sw, oret, ogot,
    in_sem, sink_sem, s1_send, s1_recv, ring_send, ring_recv, t_send, t_recv, o_send, o_recv,
):
    tm = lax.axis_index("tm")
    op = lax.axis_index("op")
    core = tm % 2
    x = (tm // 2) % 4
    y = op // 2
    z = (op % 2) * 4 + tm // 8

    def dev(x_, y_, z_, c_):
        return ((z_ % 4) * 8 + x_ * 2 + c_, y_ * 2 + z_ // 4)

    def block_of(x_, y_):
        p = (x_ + 4 - y_) % 4
        return y_ % 2 + 2 * (p // 2), p % 2

    cp_src = pltpu.make_async_copy(src_ref, src_v, in_sem.at[0])
    cp_per = pltpu.make_async_copy(peram_ref.at[0], per_v, in_sem.at[1])
    cp_src.start()
    cp_per.start()
    cp_sink = [
        pltpu.make_async_copy(sink_ref.at[0, pl.ds(4 * g, 4)], sink_v.at[pl.ds(4 * g, 4)], sink_sem.at[g])
        for g in range(GROUPS)
    ]
    for cp in cp_sink:
        cp.start()

    barrier = pltpu.get_barrier_semaphore()

    @pl.loop(1, 32)
    def _(k):
        pl.semaphore_signal(
            barrier, inc=1,
            device_id=dev((x + k // 2) % 4, (y + k // 8) % 4, z, (core + k) % 2),
            device_id_type=MESH,
        )

    z_up = (z + 1) % 8
    z_dn = (z + 7) % 8
    for z_n in (z_up, z_dn):
        pl.semaphore_signal(barrier, inc=1, device_id=dev(x, y, z_n, core), device_id_type=MESH)

    cp_per.wait()
    pr = per_v[0].astype(F32)
    pi = per_v[1].astype(F32)
    prt = pr.T.astype(BF)
    pit = pi.T
    left[0:256, 0:256] = prt
    left[256:512, 256:512] = prt
    left[256:512, 0:256] = pit.astype(BF)
    left[0:256, 256:512] = (-pit).astype(BF)
    row = lax.broadcasted_iota(jnp.int32, (256, 256), 0) < 128
    col = lax.broadcasted_iota(jnp.int32, (256, 256), 1) < 128
    flip = jnp.where(row == col, 1.0, -1.0).astype(F32)
    br = (pr * flip).astype(BF)
    bi = -(pi * flip)
    bar[0:256, 0:256] = br
    bar[256:512, 256:512] = br
    bar[0:256, 256:512] = bi.astype(BF)
    bar[256:512, 0:256] = (-bi).astype(BF)

    cp_src.wait()
    pl.semaphore_wait(barrier, 33)

    me8 = x * 2 + core
    first = []
    for r in range(2):
        for far in range(2):
            xd = (2 * (y // 2) + r + y + 2 * far) % 4
            yd = (y + 2 * far) % 4
            for lh in range(2):
                src = src_v.at[:, :, pl.ds(16 * r, 16), pl.ds(128 * lh, 128)]
                dst = sring.at[0, me8]
                k = (r * 2 + far) * 2 + lh
                cp = pltpu.make_async_remote_copy(
                    src, dst, s1_send.at[k], s1_recv.at[me8],
                    device_id=dev(xd, yd, z, lh), device_id_type=MESH,
                )
                if far:
                    cp.start()
                    first.append((cp, None))
                else:
                    mine = jnp.logical_and(xd == x, core == lh)

                    @pl.when(jnp.logical_not(mine))
                    def _():
                        cp.start()

                    @pl.when(mine)
                    def _():
                        pltpu.make_async_copy(src, dst, s1_recv.at[me8]).start()

                    first.append((cp, jnp.logical_not(mine)))

    def ring(slot_from, slot_to, z_n, ch):
        return pltpu.make_async_remote_copy(
            sring.at[slot_from, pl.ds(4 * ch, 4)], sring.at[slot_to, pl.ds(4 * ch, 4)],
            ring_send.at[slot_from, ch] if z_n is z_up else ring_send.at[8 + slot_from, ch],
            ring_recv.at[slot_to, ch],
            device_id=dev(x, y, z_n, core), device_id_type=MESH,
        )

    ring_cps = []

    def ring_step(k, ch):
        up_from, dn_from = k - 1, (9 - k) % 8
        if k > 1:
            if k < 4 or ch == 0:
                ring_wait(up_from, ch)
            if k < 4 or ch == 1:
                ring_wait(dn_from, ch)
        if k < 4 or ch == 0:
            cp = ring(up_from, k, z_up, ch)
            cp.start()
            ring_cps.append(cp)
        if k < 4 or ch == 1:
            cp = ring(dn_from, 8 - k, z_dn, ch)
            cp.start()
            ring_cps.append(cp)

    waited = set()

    def ring_wait(slot, ch):
        if (slot, ch) in waited:
            return
        waited.add((slot, ch))
        ref = sring.at[slot, pl.ds(4 * ch, 4)]
        pltpu.make_async_copy(ref, ref, ring_recv.at[slot, ch]).wait()

    def place_source(d, ch):
        zs = (z + 8 - d) % 8
        h = zs // 4
        zl = zs % 4

        @pl.loop(0, 4)
        def _(s):
            for j in range(3):
                for c in range(2):
                    tile = sring[d, 4 * ch + s, j, c].astype(F32)
                    fs[h, zl, pl.ds(c * 24 + (4 * ch + s) * 3 + j, 16, STRIDE_S), :] = tile

    def turned(g):
        cp_sink[g].wait()

        @pl.loop(0, 4)
        def _(i4):
            i = 4 * g + i4
            prod = dot_t(left[:, 0:256], sink_v[i, 0]) + dot_t(left[:, 256:512], sink_v[i, 1])
            prod = prod.astype(BF)
            prod = jnp.concatenate([prod[0:256], prod[256:512]], axis=1)
            turn = jnp.dot(prod, bar[...], preferred_element_type=F32).astype(BF)
            for ys in range(4):
                for h in range(2):
                    for r in range(2):
                        b0 = ys * 64 + h * 32 + r * 16
                        for c in range(2):
                            for lh in range(2):
                                tout[ys, r, lh, g, c * 4 + i4, h] = turn[
                                    b0:b0 + 16, c * 256 + lh * 128:c * 256 + lh * 128 + 128
                                ]

    t_cps = []
    my_ys, my_r = block_of(x, y)

    def send_turned(g):
        for cls in range(7, -1, -1):
            if cls == 0:
                cp = pltpu.make_async_remote_copy(
                    tout.at[my_ys, my_r, 1 - core, g], recv.at[core, g],
                    t_send.at[g, 0], t_recv.at[core, g],
                    device_id=dev(x, y, z, 1 - core), device_id_type=MESH,
                )
                cp.start()
                t_cps.append(cp)
                pltpu.make_async_copy(tout.at[my_ys, my_r, core, g], recv.at[core, g], t_recv.at[core, g]).start()
                continue
            for lh in range(2):
                dx, dy = HOPS[cls][(g + lh) % 2]
                xd, yd = (x + dx) % 4, (y + dy) % 4
                ys, r = block_of(xd, yd)
                cp = pltpu.make_async_remote_copy(
                    tout.at[ys, r, lh, g], recv.at[2 * cls + core, g],
                    t_send.at[g, 2 * cls + lh], t_recv.at[2 * cls + core, g],
                    device_id=dev(xd, yd, z, lh), device_id_type=MESH,
                )
                cp.start()
                t_cps.append(cp)

    turned(0)
    send_turned(0)
    for k in range(8):
        ref = sring.at[0, k]
        pltpu.make_async_copy(ref, ref, s1_recv.at[k]).wait()
    ring_step(1, 0)
    ring_step(1, 1)
    turned(1)
    send_turned(1)
    place_source(0, 0)
    place_source(0, 1)
    turned(2)
    send_turned(2)
    for k in range(2, 5):
        for ch in range(2):
            ring_step(k, ch)
            if k < 4 or ch == 0:
                place_source(k - 1, ch)
            if k < 4 or ch == 1:
                place_source(9 - k, ch)
    for slot, ch in ((3, 1), (5, 0), (4, 0), (4, 1)):
        ring_wait(slot, ch)
        place_source(slot, ch)

    @pl.loop(0, 16)
    def _(b):
        for h in range(2):
            for c in range(2):
                rows = [fs[h, zl, pl.ds(b * STRIDE_S + c * 24, 24), :] for zl in range(4)]
                rows.append(jnp.zeros((32, 128), F32))
                sw[b, c * 128:c * 128 + 128, h * 128:h * 128 + 128] = jnp.concatenate(rows, axis=0).astype(BF)

    sign = jnp.where(lax.broadcasted_iota(jnp.int32, (16, 8, 128), 1) < 4, -1.0, 1.0).astype(F32)
    o_cps = []
    for g in range(GROUPS):
        for slot in range(16):
            ref = recv.at[slot, g]
            pltpu.make_async_copy(ref, ref, t_recv.at[slot, g]).wait()

        @pl.loop(0, 16)
        def _(slot):
            for ci in range(8):
                for h in range(2):
                    tile = recv[slot, g, ci, h].astype(F32)
                    ft[h, pl.ds(slot * 8 + ci, 16, STRIDE_T), :] = tile

        def step(b, acc):
            lhs = jnp.concatenate([ft[h, pl.ds(b * STRIDE_T, 128), :] for h in range(2)], axis=1).astype(BF)
            return acc + dot_t(lhs, sw[b])

        acc = lax.fori_loop(0, 16, step, jnp.zeros((128, 256), F32))
        a_re = acc[:, 0:128].reshape(16, 8, 128)
        a_im = acc[:, 128:256].reshape(16, 8, 128)
        oret[g] = a_re + sign * jnp.concatenate([a_im[:, 4:8], a_im[:, 0:4]], axis=1)

        for cls in range(8):
            if cls == 0:
                cp = pltpu.make_async_remote_copy(
                    oret.at[g, 1 - core], ogot.at[g, core], o_send.at[g, 0], o_recv.at[g, core],
                    device_id=dev(x, y, z, 1 - core), device_id_type=MESH,
                )
                cp.start()
                o_cps.append(cp)
                continue
            (dx0, dy0), (dx1, dy1) = HOPS[cls]
            odd = (g + core) % 2
            dx = dx0 + odd * (dx1 - dx0)
            dy = dy0 + odd * (dy1 - dy0)
            xd, yd = (x + 4 - dx) % 4, (y + 4 - dy) % 4
            for cs in range(2):
                cp = pltpu.make_async_remote_copy(
                    oret.at[g, 2 * cls + cs], ogot.at[g, 2 * cls + core],
                    o_send.at[g, 2 * cls + cs], o_recv.at[g, 2 * cls + core],
                    device_id=dev(xd, yd, z, cs), device_id_type=MESH,
                )
                cp.start()
                o_cps.append(cp)

    for g in range(GROUPS):
        for slot in range(2, 16):
            ref = ogot.at[g, slot]
            pltpu.make_async_copy(ref, ref, o_recv.at[g, slot]).wait()
        ref = ogot.at[g, 1 - core]
        pltpu.make_async_copy(ref, ref, o_recv.at[g, 1 - core]).wait()
        total = oret[g, core] + ogot[g, 1 - core]
        for slot in range(2, 16):
            total = total + ogot[g, slot]
        for c in range(2):
            out_ref[c, 4 * g:4 * g + 4, :] = total[4 * c:4 * c + 4, 0:96]

    for cp, cond in first:
        if cond is None:
            cp.wait_send()
        else:
            @pl.when(cond)
            def _():
                cp.wait_send()
    for cp in ring_cps + t_cps + o_cps:
        cp.wait_send()


def local(peram, sink_elementals, source_elementals, irrep):
    group_ops = sink_elementals.shape[1]
    dma = pltpu.SemaphoreType.DMA
    full = pl.pallas_call(
        kernel,
        out_shape=jax.ShapeDtypeStruct((2, 12, 96), F32),
        in_specs=[pl.BlockSpec(memory_space=pl.ANY)] * 3,
        out_specs=pl.BlockSpec(memory_space=pltpu.VMEM),
        scratch_shapes=[
            pltpu.VMEM((2, 256, 256), BF),
            pltpu.VMEM((12, 2, 256, 256), BF),
            pltpu.VMEM((3, 2, 32, 256), BF),
            pltpu.VMEM((512, 512), BF),
            pltpu.VMEM((512, 512), BF),
            pltpu.VMEM((4, 2, 2, 3, 8, 2, 16, 128), BF),
            pltpu.VMEM((16, 3, 8, 2, 16, 128), BF),
            pltpu.VMEM((8, 8, 3, 2, 16, 128), BF),
            pltpu.VMEM((2, 4, 16 * STRIDE_S, 128), F32),
            pltpu.VMEM((2, 16 * STRIDE_T, 128), F32),
            pltpu.VMEM((16, 256, 256), BF),
            pltpu.VMEM((3, 16, 8, 128), F32),
            pltpu.VMEM((3, 16, 8, 128), F32),
            dma((2,)),
            dma((3,)),
            dma((8,)),
            dma((8,)),
            dma((16, 2)),
            dma((8, 2)),
            dma((3, 16)),
            dma((16, 3)),
            dma((3, 16)),
            dma((3, 16)),
        ],
        compiler_params=pltpu.CompilerParams(
            collective_id=0, has_side_effects=True, vmem_limit_bytes=48 * 1024 * 1024
        ),
        cost_estimate=pl.CostEstimate(flops=7_000_000_000, bytes_accessed=4_000_000, transcendentals=0),
    )(peram, sink_elementals, source_elementals)
    first = lax.axis_index("op") * group_ops
    own_labels = lax.dynamic_slice_in_dim(irrep, first, group_ops, 0)
    same = (own_labels[:, None] == irrep[None, :]).astype(F32)
    return (full * same[None, :, :])[None]


def solution(mesh):
    return jax.shard_map(
        local,
        mesh=mesh,
        in_specs=(
            P("tm", None, None, None),
            P("tm", "op", None, None, None),
            P("tm", None, "op", None),
            P(),
        ),
        out_specs=P("tm", None, "op", None),
        check_vma=False,
    )
```

time: 299 us -> 67.5 us (0.23)
  waiting for transfers between devices: 127 us -> 0 us
  Pallas kernels: 0 us -> 61.5 us
  local copies, waits for them, and re-layouts: 64.6 us -> 5.07 us
  blocking collectives: 56.7 us -> 0 us
  matrix products: 35.3 us -> 0 us
  between operations: 13.5 us -> 0.02 us
    all_gather x1 -> x0, waiting for transfers between devices: 127 us -> none  [local(): whole = lax.all_gather(rows, 'tm', axis=0, tiled=True)]
    pallas_call x0 -> x1, Pallas kernels: none -> 61.5 us  [local(): pl.pallas_call(kernel, out_shape=jax.ShapeDtypeStruct((2, 12, 96), F32),...]
    all_gather x1 -> x0, blocking collectives: 56.7 us -> none  [local(): rows = lax.all_gather(source_elementals, 'op', axis=2, tiled=True)]
    dot_general x12 -> x0, matrix products: 35.3 us -> none  [the longest x1 8.61 us: pair_traces(): jnp.einsum('toba,jba->toj', turn_re, src_im, preferred_element_type=jnp.f...]
    unnamed x17 -> x6, local copies, waits for them, and re-layouts: 37.6 us -> 3.73 us
    slice x1 -> x0, local copies, waits for them, and re-layouts: 17.4 us -> none  [local(): mine = pair_traces(turn_re, turn_im, whole[:, 0], whole[:, 1])]
    convert_element_type x2 -> x0, local copies, waits for them, and re-layouts: 8.02 us -> none  [the longest x1 4.51 us: local(): turn_re = turn_re.astype(jnp.bfloat16)]
  transfers between devices with their start and end apart: 1 -> 0, of which waited for: 1 -> 0; matrix products, arithmetic and copies ran while one was open for 6% -> 0% of each run, Pallas kernels for 0% -> 0%
where the time goes in v1:
time: 67.5 us; the launch traced here: 67.3 us
  Pallas kernels  61.5 us (91%)
  local copies, waits for them, and re-layouts  5.07 us (8%)
  other arithmetic  0.73 us (1%)
    pallas_call x1, Pallas kernels, local(): pl.pallas_call(kernel, out_shape=jax.ShapeDtypeStruct((2, 12, 96), F32),...  61.5 us
    unnamed x6, local copies, waits for them, and re-layouts  3.73 us

profile of v1, /device:TPU:1, one launch (start us, length us, event | category | flops | bytes accessed | tf_op | source)
XLA Modules:
  0.0 67.3 jit_solution(17675877199958629595)
XLA Ops:
  0.0 0.7 %dynamic_slice.3 = s32[12]{0:T(128)S(1)} dynamic-slice(s32[96]{0:T(128)} %param.7, s32[]{:T(128)S(6)} %select_n.3), dynamic_slice_sizes={12} | dynamic-slice | bytes 100 | tf_op jit(solution)/shard_map/dynamic_slice | solution.py:362
  0.7 0.7 %compare_convert_fusion = f32[12,96]{1,0:T(8,128)S(1)} fusion(s32[96]{0:T(128)} %param.7, s32[12]{0:T(128)S(1)} %dynamic_slice.3), kind=kLoop, calls=%fused_computation.1 | loop fusion | flops 2304 | bytes 5040 | tf_op jit(solution)/shard_map/convert_element_type | solution.py:363
  1.5 0.0 copy-start
  1.5 1.9 %copy-done = bf16[1,12,2,256,256]{4,3,2,1,0:T(8,128)(2,1)S(1)} copy-done((bf16[1,12,2,256,256]{4,3,2,1,0:T(8,128)(2,1)S(1)}, bf16[1,12,2,256,256]{4,3,2,1,0:T(8,128)(2,1)}, u32[]{:S(2)}) %copy-start) | copy-done | bytes 3145752
  3.3 0.0 copy-start.1
  3.3 0.9 %copy-done.1 = bf16[1,2,256,256]{3,2,1,0:T(8,128)(2,1)S(1)} copy-done((bf16[1,2,256,256]{3,2,1,0:T(8,128)(2,1)S(1)}, bf16[1,2,256,256]{3,2,1,0:T(8,128)(2,1)}, u32[]{:S(2)}) %copy-start.1) | copy-done | bytes 262168
  4.3 0.0 copy-start.2
  4.3 0.9 %copy-done.2 = bf16[3,2,32,256]{3,2,1,0:T(8,128)(2,1)S(1)} copy-done((bf16[3,2,32,256]{3,2,1,0:T(8,128)(2,1)S(1)}, bf16[3,2,32,256]{3,2,1,0:T(8,128)(2,1)}, u32[]{:S(2)}) %copy-start.2) | copy-done | bytes 98328
  5.2 61.5 %shard_map.46 = f32[2,12,96]{2,1,0:T(8,128)S(1)} custom-call(bf16[1,2,256,256]{3,2,1,0:T(8,128)(2,1)S(1)} %copy-done.1, bf16[1,12,2,256,256]{4,3,2,1,0:T(8,128)(2,1)S(1)} %copy-done, bf16[3,2,32,256]{3,2,1,0:T(8,128)(2,1)S(1)} %copy-done.2), custom_call_target="tpu_custom_call" | custom-call | flops 7000000000 | bytes 4000000 | tf_op jit(solution)/shard_map/pallas_call | solution.py:326
  66.7 0.6 copy.5
  (1 shorter events, 0.0 us)
Async XLA Ops:
  1.5 1.9 %copy-start = (bf16[1,12,2,256,256]{4,3,2,1,0:T(8,128)(2,1)S(1)}, bf16[1,12,2,256,256]{4,3,2,1,0:T(8,128)(2,1)}, u32[]{:S(2)}) copy-start(bf16[1,12,2,256,256]{4,3,2,1,0:T(8,128)(2,1)} %sink_ref.1) | copy-start | bytes 9437188
  3.3 0.9 %copy-start.1 = (bf16[1,2,256,256]{3,2,1,0:T(8,128)(2,1)S(1)}, bf16[1,2,256,256]{3,2,1,0:T(8,128)(2,1)}, u32[]{:S(2)}) copy-start(bf16[1,2,256,256]{3,2,1,0:T(8,128)(2,1)} %peram_ref.1) | copy-start | bytes 786436
  4.3 0.9 %copy-start.2 = (bf16[3,2,32,256]{3,2,1,0:T(8,128)(2,1)S(1)}, bf16[3,2,32,256]{3,2,1,0:T(8,128)(2,1)}, u32[]{:S(2)}) copy-start(bf16[3,2,32,256]{3,2,1,0:T(8,128)(2,1)} %src_ref.1) | copy-start | bytes 294916

commit v2 on v1

v2 whole, which is shorter than its diff:
```python
import jax
import jax.numpy as jnp
from jax import lax
from jax.experimental import pallas as pl
from jax.experimental.pallas import tpu as pltpu
from jax.sharding import PartitionSpec as P

MESH = pl.DeviceIdType.MESH
BF = jnp.bfloat16
F32 = jnp.float32
GROUPS = 3
STRIDE_T = 136
STRIDE_S = 48

HOPS = (
    ((0, 0), (0, 0)),
    ((1, 0), (1, 0)),
    ((3, 0), (3, 0)),
    ((0, 1), (0, 1)),
    ((0, 3), (0, 3)),
    ((3, 3), (1, 1)),
    ((1, 3), (3, 1)),
    ((2, 0), (0, 2)),
)


def dot_t(a, b):
    return lax.dot_general(a, b, (((1,), (1,)), ((), ())), preferred_element_type=F32)


def kernel(
    peram_ref, sink_ref, src_ref, lab_ref, out_ref,
    per_v, sink_v, src_v, lab_v, left, bar, tout, recv, sring, fs, ft, lhs, sw, oret, ogot,
    in_sem, sink_sem, s1_send, s1_recv, ring_send, ring_recv, t_send, t_recv, o_send, o_recv, answer,
):
    tm = lax.axis_index("tm")
    op = lax.axis_index("op")
    core = tm % 2
    x = (tm // 2) % 4
    y = op // 2
    z = (op % 2) * 4 + tm // 8

    def dev(x_, y_, z_, c_):
        return ((z_ % 4) * 8 + x_ * 2 + c_, y_ * 2 + z_ // 4)

    def block_of(x_, y_):
        p = (x_ + 4 - y_) % 4
        return y_ % 2 + 2 * (p // 2), p % 2

    cp_src = pltpu.make_async_copy(src_ref, src_v, in_sem.at[0])
    cp_per = pltpu.make_async_copy(peram_ref.at[0], per_v, in_sem.at[1])
    cp_lab = pltpu.make_async_copy(lab_ref, lab_v, in_sem.at[2])
    cp_src.start()
    cp_per.start()
    cp_lab.start()
    cp_sink = [
        pltpu.make_async_copy(sink_ref.at[0, pl.ds(4 * g, 4)], sink_v.at[pl.ds(4 * g, 4)], sink_sem.at[g])
        for g in range(GROUPS)
    ]
    for cp in cp_sink:
        cp.start()

    barrier = pltpu.get_barrier_semaphore()

    @pl.loop(1, 32)
    def _(k):
        pl.semaphore_signal(
            barrier, inc=1,
            device_id=dev((x + k // 2) % 4, (y + k // 8) % 4, z, (core + k) % 2),
            device_id_type=MESH,
        )

    z_up = (z + 1) % 8
    z_dn = (z + 7) % 8
    later_up = z < 7
    later_dn = z == 0
    for z_n, later in ((z_up, later_up), (z_dn, later_dn)):
        @pl.when(later)
        def _():
            pl.semaphore_signal(barrier, inc=1, device_id=dev(x, y, z_n, core), device_id_type=MESH)

    def turned(g):
        cp_sink[g].wait()
        prods = []
        for i4 in range(4):
            i = 4 * g + i4
            elem = jnp.concatenate([sink_v[i, 0], sink_v[i, 1]], axis=1)
            prod = dot_t(left[...], elem).astype(BF)
            prods.append(jnp.concatenate([prod[0:256], prod[256:512]], axis=1))
        for i4 in range(4):
            turn = jnp.dot(prods[i4], bar[...], preferred_element_type=F32).astype(BF)
            for ys in range(4):
                for h in range(2):
                    for r in range(2):
                        b0 = ys * 64 + h * 32 + r * 16
                        for c in range(2):
                            for lh in range(2):
                                tout[ys, r, lh, g, c * 4 + i4, h] = turn[
                                    b0:b0 + 16, c * 256 + lh * 128:c * 256 + lh * 128 + 128
                                ]

    cp_src.wait()
    pl.semaphore_wait(barrier, 31 + jnp.where(z > 0, 1, 0) + jnp.where(z == 7, 1, 0))
    for z_n, later, at in ((z_up, later_up, 1), (z_dn, later_dn, 0)):
        @pl.when(jnp.logical_not(later))
        def _():
            pl.semaphore_signal(answer.at[at], inc=1, device_id=dev(x, y, z_n, core), device_id_type=MESH)

    first = []
    for r in range(2):
        for far in range(2):
            xd = (2 * (y // 2) + r + y + 2 * far) % 4
            yd = (y + 2 * far) % 4
            for lh in range(2):
                src = src_v.at[:, :, pl.ds(16 * r, 16), pl.ds(128 * lh, 128)]
                me8 = ((x + 4 - xd) % 4) * 2 + core
                dst = sring.at[0, me8]
                k = (r * 2 + far) * 2 + lh
                cp = pltpu.make_async_remote_copy(
                    src, dst, s1_send.at[k], s1_recv.at[me8],
                    device_id=dev(xd, yd, z, lh), device_id_type=MESH,
                )
                if far:
                    cp.start()
                    first.append((cp, None))
                else:
                    mine = jnp.logical_and(xd == x, core == lh)

                    @pl.when(jnp.logical_not(mine))
                    def _():
                        cp.start()

                    @pl.when(mine)
                    def _():
                        pltpu.make_async_copy(src, dst, s1_recv.at[me8]).start()

                    first.append((cp, jnp.logical_not(mine)))

    def ring(slot_from, slot_to, z_n, ch):
        return pltpu.make_async_remote_copy(
            sring.at[slot_from, pl.ds(2 * ch, 2)], sring.at[slot_to, pl.ds(2 * ch, 2)],
            ring_send.at[slot_from, ch] if z_n is z_up else ring_send.at[8 + slot_from, ch],
            ring_recv.at[slot_to, ch],
            device_id=dev(x, y, z_n, core), device_id_type=MESH,
        )

    ring_cps = []

    def ring_step(k, ch):
        up_from, dn_from = k - 1, (9 - k) % 8
        if k < 4:
            ring_wait(up_from, ch)
            cp = ring(up_from, k, z_up, ch)
            cp.start()
            ring_cps.append(cp)
        ring_wait(dn_from, ch)
        cp = ring(dn_from, 8 - k, z_dn, ch)
        cp.start()
        ring_cps.append(cp)

    waited = set()

    def ring_wait(slot, ch):
        if (slot, ch) in waited:
            return
        waited.add((slot, ch))
        if slot == 0:
            for k in (2 * ch, 2 * ch + 1):
                ref = sring.at[0, k]
                pltpu.make_async_copy(ref, ref, s1_recv.at[k]).wait()
            return
        ref = sring.at[slot, pl.ds(2 * ch, 2)]
        pltpu.make_async_copy(ref, ref, ring_recv.at[slot, ch]).wait()

    def place_source(d):
        zs = (z + 8 - d) % 8
        h = zs // 4
        zl = zs % 4

        @pl.loop(0, 4)
        def _(ch):
            xs = (x + ch) % 4
            for cs in range(2):
                for j in range(3):
                    for c in range(2):
                        tile = sring[d, 2 * ch + cs, j, c].astype(F32)
                        fs[h, zl, pl.ds(xs * 6 + c * 24 + cs * 3 + j, 16, STRIDE_S), :] = tile

        for b in range(16):
            sw[h, b, zl] = fs[h, zl, pl.ds(b * STRIDE_S, 48), :].astype(BF)

    t_cps = []
    my_ys, my_r = block_of(x, y)

    def send_turned(g):
        for cls in range(7, -1, -1):
            if cls == 0:
                cp = pltpu.make_async_remote_copy(
                    tout.at[my_ys, my_r, 1 - core, g], recv.at[core, g],
                    t_send.at[g, 0], t_recv.at[core, g],
                    device_id=dev(x, y, z, 1 - core), device_id_type=MESH,
                )
                cp.start()
                t_cps.append(cp)
                pltpu.make_async_copy(tout.at[my_ys, my_r, core, g], recv.at[core, g], t_recv.at[core, g]).start()
                continue
            for lh in range(2):
                dx, dy = HOPS[cls][(g + lh) % 2]
                xd, yd = (x + dx) % 4, (y + dy) % 4
                ys, r = block_of(xd, yd)
                cp = pltpu.make_async_remote_copy(
                    tout.at[ys, r, lh, g], recv.at[2 * cls + core, g],
                    t_send.at[g, 2 * cls + lh], t_recv.at[2 * cls + core, g],
                    device_id=dev(xd, yd, z, lh), device_id_type=MESH,
                )
                cp.start()
                t_cps.append(cp)

    def gather_rows(g):
        @pl.loop(0, 8)
        def _(k):
            cls = (8 - k) % 8
            for cs in range(2):
                ref = recv.at[2 * cls + cs, g]
                pltpu.make_async_copy(ref, ref, t_recv.at[2 * cls + cs, g]).wait()
                for ci in range(8):
                    for h in range(2):
                        tile = recv[2 * cls + cs, g, ci, h].astype(F32)
                        ft[h, pl.ds(cls * 16 + cs * 8 + ci, 16, STRIDE_T), :] = tile
            for b in range(16):
                for h in range(2):
                    tile = ft[h, pl.ds(b * STRIDE_T + cls * 16, 16), :]
                    lhs[b, pl.ds(g * 128 + cls * 16, 16), h * 128:h * 128 + 128] = tile.astype(BF)

    cp_per.wait()
    pr = per_v[0].astype(F32)
    pi = per_v[1].astype(F32)
    prt = pr.T.astype(BF)
    pit = pi.T
    left[0:256, 0:256] = prt
    left[256:512, 256:512] = prt
    left[256:512, 0:256] = pit.astype(BF)
    left[0:256, 256:512] = (-pit).astype(BF)
    row = lax.broadcasted_iota(jnp.int32, (256, 256), 0) < 128
    col = lax.broadcasted_iota(jnp.int32, (256, 256), 1) < 128
    flip = jnp.where(row == col, 1.0, -1.0).astype(F32)
    br = (pr * flip).astype(BF)
    bi = -(pi * flip)
    bar[0:256, 0:256] = br
    bar[256:512, 256:512] = br
    bar[0:256, 256:512] = bi.astype(BF)
    bar[256:512, 0:256] = (-bi).astype(BF)

    turned(0)
    for later, at in ((later_up, 0), (later_dn, 1)):
        @pl.when(later)
        def _():
            pl.semaphore_wait(answer.at[at], 1)
    ring_step(1, 0)
    send_turned(0)
    for ch in range(1, 4):
        ring_step(1, ch)
    turned(1)
    send_turned(1)
    place_source(0)
    ring_step(2, 0)
    ring_step(2, 1)
    turned(2)
    send_turned(2)
    ring_step(2, 2)
    ring_step(2, 3)
    place_source(1)
    place_source(7)
    for ch in range(4):
        ring_step(3, ch)
    place_source(2)
    place_source(6)
    gather_rows(0)
    for ch in range(4):
        ring_step(4, ch)
    gather_rows(1)
    for slot in (5, 3, 4):
        for ch in range(4):
            ring_wait(slot, ch)
        place_source(slot)

    cp_lab.wait()
    labels = jnp.broadcast_to(lab_v[...].astype(F32), (8, 96))
    lane = lax.broadcasted_iota(jnp.int32, (8, 96), 1)
    sub = lax.broadcasted_iota(jnp.int32, (8, 96), 0) % 4
    same = []
    for g in range(GROUPS):
        own = jnp.sum(jnp.where(lane == op * 12 + 4 * g + sub, labels, 0.0), axis=1, keepdims=True)
        same.append((own == labels).astype(F32))

    o_cps = []

    def contract(g0, n):
        rows = n * 128
        acc = None
        for b in range(16):
            right = jnp.concatenate([sw[0, b].reshape(192, 128), sw[1, b].reshape(192, 128)], axis=1)
            part = dot_t(lhs[b, g0 * 128:g0 * 128 + rows, :], right)
            acc = part if acc is None else acc + part
        acc = jnp.concatenate([acc, jnp.zeros((rows, 64), F32)], axis=1)
        other = pltpu.roll(acc, 232, 1).reshape(n * 16, 8, 256)
        sign = jnp.where(lax.broadcasted_iota(jnp.int32, (n * 16, 8, 256), 1) < 4, -1.0, 1.0).astype(F32)
        other = jnp.concatenate([other[:, 4:8], other[:, 0:4]], axis=1)
        oret[g0:g0 + n] = (acc.reshape(n * 16, 8, 256) + sign * other).reshape(n, 16, 8, 256)

    def give_back(gs, cls):
        g = gs[0]
        part = pl.ds(g, len(gs))
        if cls == 0:
            cp = pltpu.make_async_remote_copy(
                oret.at[part, 1 - core], ogot.at[part, core], o_send.at[g, 0], o_recv.at[g, core],
                device_id=dev(x, y, z, 1 - core), device_id_type=MESH,
            )
            cp.start()
            o_cps.append(cp)
            return
        (dx0, dy0), (dx1, dy1) = HOPS[cls]
        odd = (g + core) % 2
        dx = dx0 + odd * (dx1 - dx0)
        dy = dy0 + odd * (dy1 - dy0)
        xd, yd = (x + 4 - dx) % 4, (y + 4 - dy) % 4
        for cs in range(2):
            cp = pltpu.make_async_remote_copy(
                oret.at[part, 2 * cls + cs], ogot.at[part, 2 * cls + core],
                o_send.at[g, 2 * cls + cs], o_recv.at[g, 2 * cls + core],
                device_id=dev(xd, yd, z, cs), device_id_type=MESH,
            )
            cp.start()
            o_cps.append(cp)

    def got_back(gs, slot):
        ref = ogot.at[pl.ds(gs[0], len(gs)), slot]
        pltpu.make_async_copy(ref, ref, o_recv.at[gs[0], slot]).wait()

    def total(g):
        out = oret[g, core] + ogot[g, 1 - core]
        for slot in range(2, 16):
            out = out + ogot[g, slot]
        out = jnp.concatenate([out[:, 48 * k:48 * k + 24] for k in range(4)], axis=1) * same[g]
        for c in range(2):
            for i4 in range(4):
                out_ref[4 * g + i4, c:c + 1, :] = out[4 * c + i4:4 * c + i4 + 1, :]

    def pairs(cls):
        return ((0, 1),) if cls < 5 else ((0,), (1,))

    contract(0, 2)
    for cls in range(7, -1, -1):
        for gs in pairs(cls):
            give_back(gs, cls)
    gather_rows(2)
    contract(2, 1)
    for cls in range(7, -1, -1):
        give_back((2,), cls)
    for cls in range(1, 8):
        for gs in pairs(cls):
            for cs in range(2):
                got_back(gs, 2 * cls + cs)
    got_back((0, 1), 1 - core)
    total(0)
    total(1)
    for slot in range(2, 16):
        got_back((2,), slot)
    got_back((2,), 1 - core)
    total(2)

    for cp, cond in first:
        if cond is None:
            cp.wait_send()
        else:
            @pl.when(cond)
            def _():
                cp.wait_send()
    for cp in ring_cps + t_cps + o_cps:
        cp.wait_send()


def local(peram, sink_elementals, source_elementals, irrep):
    dma = pltpu.SemaphoreType.DMA
    full = pl.pallas_call(
        kernel,
        out_shape=jax.ShapeDtypeStruct((12, 2, 96), F32),
        in_specs=[pl.BlockSpec(memory_space=pl.ANY)] * 4,
        out_specs=pl.BlockSpec(memory_space=pltpu.VMEM),
        scratch_shapes=[
            pltpu.VMEM((2, 256, 256), BF),
            pltpu.VMEM((12, 2, 256, 256), BF),
            pltpu.VMEM((3, 2, 32, 256), BF),
            pltpu.VMEM((1, 96), jnp.int32),
            pltpu.VMEM((512, 512), BF),
            pltpu.VMEM((512, 512), BF),
            pltpu.VMEM((4, 2, 2, 3, 8, 2, 16, 128), BF),
            pltpu.VMEM((16, 3, 8, 2, 16, 128), BF),
            pltpu.VMEM((8, 8, 3, 2, 16, 128), BF),
            pltpu.VMEM((2, 4, 16 * STRIDE_S, 128), F32),
            pltpu.VMEM((2, 16 * STRIDE_T, 128), F32),
            pltpu.VMEM((16, 384, 256), BF),
            pltpu.VMEM((2, 16, 4, 48, 128), BF),
            pltpu.VMEM((3, 16, 8, 256), F32),
            pltpu.VMEM((3, 16, 8, 256), F32),
            dma((3,)),
            dma((3,)),
            dma((8,)),
            dma((8,)),
            dma((16, 4)),
            dma((8, 4)),
            dma((3, 16)),
            dma((16, 3)),
            dma((3, 16)),
            dma((3, 16)),
            pltpu.SemaphoreType.REGULAR((2,)),
        ],
        compiler_params=pltpu.CompilerParams(
            collective_id=0, has_side_effects=True, vmem_limit_bytes=60 * 1024 * 1024
        ),
        cost_estimate=pl.CostEstimate(flops=7_000_000_000, bytes_accessed=4_000_000, transcendentals=0),
    )(peram, sink_elementals, source_elementals, irrep.reshape(1, 96))
    return jnp.swapaxes(full, 0, 1)[None]


def solution(mesh):
    return jax.shard_map(
        local,
        mesh=mesh,
        in_specs=(
            P("tm", None, None, None),
            P("tm", "op", None, None, None),
            P("tm", None, "op", None),
            P(),
        ),
        out_specs=P("tm", None, "op", None),
        check_vma=False,
    )
```

time: 67.5 us -> 49.6 us (0.73)
  Pallas kernels: 61.5 us -> 48.1 us
  local copies, waits for them, and re-layouts: 5.07 us -> 1.31 us
  other arithmetic: 0.73 us -> 0 us
    pallas_call x1, Pallas kernels: 61.5 us -> 48.1 us  [local(): pl.pallas_call(kernel, out_shape=jax.ShapeDtypeStruct((12, 2, 96), F32),...]
    unnamed x6 -> x1, local copies, waits for them, and re-layouts: 3.73 us -> 1.31 us
    dynamic_slice x1 -> x0, local copies, waits for them, and re-layouts: 0.73 us -> none  [local(): own_labels = lax.dynamic_slice_in_dim(irrep, first, group_ops, 0)]
    convert_element_type x1 -> x0, other arithmetic: 0.72 us -> none  [local(): same = (own_labels[:, None] == irrep[None, :]).astype(F32)]
where the time goes in v2:
time: 49.6 us; the launch traced here: 49.5 us
  Pallas kernels  48.1 us (97%)
  local copies, waits for them, and re-layouts  1.31 us (3%)
    pallas_call x1, Pallas kernels, local(): pl.pallas_call(kernel, out_shape=jax.ShapeDtypeStruct((12, 2, 96), F32),...  48.1 us
    unnamed x1, local copies, waits for them, and re-layouts  1.31 us

profile of v2, /device:TPU:1, one launch (start us, length us, event | category | flops | bytes accessed | tf_op | source)
XLA Modules:
  0.0 49.5 jit_solution(9829898413667178902)
XLA Ops:
  0.0 48.1 %shard_map.46 = f32[12,2,96]{2,1,0:T(2,128)} custom-call(bf16[1,2,256,256]{3,2,1,0:T(8,128)(2,1)} %peram_ref.1, bf16[1,12,2,256,256]{4,3,2,1,0:T(8,128)(2,1)} %sink_ref.1, bf16[3,2,32,256]{3,2,1,0:T(8,128)(2,1)} %src_ref.1, s32[1,96]{1,0:T(1,128)} %bitcast.5), custom_call_target="tpu_custom_call" | custom-call | flops 7000000000 | bytes 4000000 | tf_op jit(solution)/shard_map/pallas_call | solution.py:385
  48.1 1.3 %copy.6 = f32[1,2,12,96]{3,1,2,0:T(2,128)} copy(f32[1,2,12,96]{3,1,2,0:T(2,128)} %bitcast.4) | data formatting | bytes 18432

commit v3 on v2

--- a/solution.py
+++ b/solution.py
@@ -146,17 +146,25 @@
 
     ring_cps = []
 
-    def ring_step(k, ch):
-        up_from, dn_from = k - 1, (9 - k) % 8
-        if k < 4:
-            ring_wait(up_from, ch)
-            cp = ring(up_from, k, z_up, ch)
-            cp.start()
-            ring_cps.append(cp)
-        ring_wait(dn_from, ch)
-        cp = ring(dn_from, 8 - k, z_dn, ch)
+    def ring_up(k, ch):
+        ring_wait(k - 1, ch)
+        cp = ring(k - 1, k, z_up, ch)
         cp.start()
         ring_cps.append(cp)
+
+    def ring_down(k, ch, cond=None):
+        ring_wait((9 - k) % 8, ch)
+        cp = ring((9 - k) % 8, 8 - k, z_dn, ch)
+        if cond is None:
+            cp.start()
+        else:
+            pl.when(cond)(cp.start)
+        return cp
+
+    def ring_step(k, ch):
+        ring_cps.append(ring_down(k, ch))
+        if k < 4:
+            ring_up(k, ch)
 
     waited = set()
 
@@ -186,14 +194,11 @@
                         tile = sring[d, 2 * ch + cs, j, c].astype(F32)
                         fs[h, zl, pl.ds(xs * 6 + c * 24 + cs * 3 + j, 16, STRIDE_S), :] = tile
 
-        for b in range(16):
-            sw[h, b, zl] = fs[h, zl, pl.ds(b * STRIDE_S, 48), :].astype(BF)
-
     t_cps = []
     my_ys, my_r = block_of(x, y)
 
     def send_turned(g):
-        for cls in range(7, -1, -1):
+        for cls in (0, 1, 2, 3, 4, 7, 5, 6):
             if cls == 0:
                 cp = pltpu.make_async_remote_copy(
                     tout.at[my_ys, my_r, 1 - core, g], recv.at[core, g],
@@ -205,7 +210,7 @@
                 pltpu.make_async_copy(tout.at[my_ys, my_r, core, g], recv.at[core, g], t_recv.at[core, g]).start()
                 continue
             for lh in range(2):
-                dx, dy = HOPS[cls][(g + lh) % 2]
+                dx, dy = HOPS[cls][lh]
                 xd, yd = (x + dx) % 4, (y + dy) % 4
                 ys, r = block_of(xd, yd)
                 cp = pltpu.make_async_remote_copy(
@@ -219,7 +224,7 @@
     def gather_rows(g):
         @pl.loop(0, 8)
         def _(k):
-            cls = (8 - k) % 8
+            cls = k
             for cs in range(2):
                 ref = recv.at[2 * cls + cs, g]
                 pltpu.make_async_copy(ref, ref, t_recv.at[2 * cls + cs, g]).wait()
@@ -252,21 +257,30 @@
     bar[256:512, 0:256] = (-bi).astype(BF)
 
     turned(0)
-    for later, at in ((later_up, 0), (later_dn, 1)):
-        @pl.when(later)
-        def _():
-            pl.semaphore_wait(answer.at[at], 1)
-    ring_step(1, 0)
     send_turned(0)
-    for ch in range(1, 4):
-        ring_step(1, ch)
     turned(1)
-    send_turned(1)
+
+    @pl.when(later_up)
+    def _():
+        pl.semaphore_wait(answer.at[0], 1)
+
+    for ch in range(4):
+        ring_up(1, ch)
+        ring_cps.append(ring_down(1, ch, jnp.logical_not(later_dn)))
+        if ch == 1:
+            send_turned(1)
+    turned(2)
+    send_turned(2)
+
+    @pl.when(later_dn)
+    def _():
+        pl.semaphore_wait(answer.at[1], 1)
+        for ch in range(4):
+            ring(0, 7, z_dn, ch).start()
+
     place_source(0)
     ring_step(2, 0)
     ring_step(2, 1)
-    turned(2)
-    send_turned(2)
     ring_step(2, 2)
     ring_step(2, 3)
     place_source(1)
@@ -280,6 +294,8 @@
         ring_step(4, ch)
     gather_rows(1)
     for slot in (5, 3, 4):
+        if slot == 4:
+            gather_rows(2)
         for ch in range(4):
             ring_wait(slot, ch)
         place_source(slot)
@@ -295,79 +311,60 @@
 
     o_cps = []
 
-    def contract(g0, n):
-        rows = n * 128
-        acc = None
-        for b in range(16):
-            right = jnp.concatenate([sw[0, b].reshape(192, 128), sw[1, b].reshape(192, 128)], axis=1)
-            part = dot_t(lhs[b, g0 * 128:g0 * 128 + rows, :], right)
-            acc = part if acc is None else acc + part
-        acc = jnp.concatenate([acc, jnp.zeros((rows, 64), F32)], axis=1)
-        other = pltpu.roll(acc, 232, 1).reshape(n * 16, 8, 256)
-        sign = jnp.where(lax.broadcasted_iota(jnp.int32, (n * 16, 8, 256), 1) < 4, -1.0, 1.0).astype(F32)
-        other = jnp.concatenate([other[:, 4:8], other[:, 0:4]], axis=1)
-        oret[g0:g0 + n] = (acc.reshape(n * 16, 8, 256) + sign * other).reshape(n, 16, 8, 256)
-
-    def give_back(gs, cls):
-        g = gs[0]
-        part = pl.ds(g, len(gs))
+    @pl.loop(0, 16, unroll=2)
+    def _(b):
+        for h in range(2):
+            for c in range(2):
+                rows = [fs[h, zl, pl.ds(b * STRIDE_S + c * 24, 24), :] for zl in range(4)]
+                if c == 0:
+                    rows.append(jnp.zeros((32, 128), F32))
+                rows = jnp.concatenate(rows, axis=0).astype(BF)
+                sw[b, c * 128:c * 128 + rows.shape[0], h * 128:h * 128 + 128] = rows
+
+    acc = dot_t(lhs[0], sw[0])
+    for b in range(1, 16):
+        acc = acc + dot_t(lhs[b], sw[b])
+    with_re = acc[:, 0:128].reshape(48, 8, 128)
+    with_im = jnp.concatenate([acc[:, 128:224], jnp.zeros((384, 32), F32)], axis=1).reshape(48, 8, 128)
+    with_im = jnp.concatenate([with_im[:, 4:8], with_im[:, 0:4]], axis=1)
+    sign = jnp.where(lax.broadcasted_iota(jnp.int32, (48, 8, 128), 1) < 4, -1.0, 1.0).astype(F32)
+    oret[...] = (with_re + sign * with_im).reshape(3, 16, 8, 128)
+
+    for cls in (7, 6, 5, 4, 3, 2, 1, 0):
         if cls == 0:
             cp = pltpu.make_async_remote_copy(
-                oret.at[part, 1 - core], ogot.at[part, core], o_send.at[g, 0], o_recv.at[g, core],
+                oret.at[:, 1 - core], ogot.at[:, core], o_send.at[0], o_recv.at[core],
                 device_id=dev(x, y, z, 1 - core), device_id_type=MESH,
             )
             cp.start()
             o_cps.append(cp)
-            return
+            continue
         (dx0, dy0), (dx1, dy1) = HOPS[cls]
-        odd = (g + core) % 2
-        dx = dx0 + odd * (dx1 - dx0)
-        dy = dy0 + odd * (dy1 - dy0)
+        dx = dx0 + core * (dx1 - dx0)
+        dy = dy0 + core * (dy1 - dy0)
         xd, yd = (x + 4 - dx) % 4, (y + 4 - dy) % 4
         for cs in range(2):
             cp = pltpu.make_async_remote_copy(
-                oret.at[part, 2 * cls + cs], ogot.at[part, 2 * cls + core],
-                o_send.at[g, 2 * cls + cs], o_recv.at[g, 2 * cls + core],
+                oret.at[:, 2 * cls + cs], ogot.at[:, 2 * cls + core],
+                o_send.at[2 * cls + cs], o_recv.at[2 * cls + core],
                 device_id=dev(xd, yd, z, cs), device_id_type=MESH,
             )
             cp.start()
             o_cps.append(cp)
 
-    def got_back(gs, slot):
-        ref = ogot.at[pl.ds(gs[0], len(gs)), slot]
-        pltpu.make_async_copy(ref, ref, o_recv.at[gs[0], slot]).wait()
-
-    def total(g):
-        out = oret[g, core] + ogot[g, 1 - core]
-        for slot in range(2, 16):
-            out = out + ogot[g, slot]
-        out = jnp.concatenate([out[:, 48 * k:48 * k + 24] for k in range(4)], axis=1) * same[g]
+    total = oret[:, core]
+    ref = ogot.at[:, 1 - core]
+    pltpu.make_async_copy(ref, ref, o_recv.at[1 - core]).wait()
+    total = total + ogot[:, 1 - core]
+    for slot in range(2, 16):
+        ref = ogot.at[:, slot]
+        pltpu.make_async_copy(ref, ref, o_recv.at[slot]).wait()
+        total = total + ogot[:, slot]
+    for g in range(GROUPS):
+        out = total[g, :, 0:96] * same[g]
         for c in range(2):
             for i4 in range(4):
                 out_ref[4 * g + i4, c:c + 1, :] = out[4 * c + i4:4 * c + i4 + 1, :]
-
-    def pairs(cls):
-        return ((0, 1),) if cls < 5 else ((0,), (1,))
-
-    contract(0, 2)
-    for cls in range(7, -1, -1):
-        for gs in pairs(cls):
-            give_back(gs, cls)
-    gather_rows(2)
-    contract(2, 1)
-    for cls in range(7, -1, -1):
-        give_back((2,), cls)
-    for cls in range(1, 8):
-        for gs in pairs(cls):
-            for cs in range(2):
-                got_back(gs, 2 * cls + cs)
-    got_back((0, 1), 1 - core)
-    total(0)
-    total(1)
-    for slot in range(2, 16):
-        got_back((2,), slot)
-    got_back((2,), 1 - core)
-    total(2)
 
     for cp, cond in first:
         if cond is None:
@@ -400,9 +397,9 @@
             pltpu.VMEM((2, 4, 16 * STRIDE_S, 128), F32),
             pltpu.VMEM((2, 16 * STRIDE_T, 128), F32),
             pltpu.VMEM((16, 384, 256), BF),
-            pltpu.VMEM((2, 16, 4, 48, 128), BF),
-            pltpu.VMEM((3, 16, 8, 256), F32),
-            pltpu.VMEM((3, 16, 8, 256), F32),
+            pltpu.VMEM((16, 224, 256), BF),
+            pltpu.VMEM((3, 16, 8, 128), F32),
+            pltpu.VMEM((3, 16, 8, 128), F32),
             dma((3,)),
             dma((3,)),
             dma((8,)),
@@ -411,8 +408,8 @@
             dma((8, 4)),
             dma((3, 16)),
             dma((16, 3)),
-            dma((3, 16)),
-            dma((3, 16)),
+            dma((16,)),
+            dma((16,)),
             pltpu.SemaphoreType.REGULAR((2,)),
         ],
         compiler_params=pltpu.CompilerParams(

time: 49.6 us -> 46 us (0.927)
  Pallas kernels: 48.1 us -> 44.6 us
    pallas_call x1, Pallas kernels: 48.1 us -> 44.6 us  [local(): pl.pallas_call(kernel, out_shape=jax.ShapeDtypeStruct((12, 2, 96), F32),...]
where the time goes in v3:
time: 46 us; the launch traced here: 45.9 us
  Pallas kernels  44.6 us (97%)
  local copies, waits for them, and re-layouts  1.31 us (3%)
    pallas_call x1, Pallas kernels, local(): pl.pallas_call(kernel, out_shape=jax.ShapeDtypeStruct((12, 2, 96), F32),...  44.6 us
    unnamed x1, local copies, waits for them, and re-layouts  1.31 us

profile of v3, /device:TPU:1, one launch (start us, length us, event | category | flops | bytes accessed | tf_op | source)
XLA Modules:
  0.0 45.9 jit_solution(1864488357221824785)
XLA Ops:
  0.0 44.6 %shard_map.46 = f32[12,2,96]{2,1,0:T(2,128)} custom-call(bf16[1,2,256,256]{3,2,1,0:T(8,128)(2,1)} %peram_ref.1, bf16[1,12,2,256,256]{4,3,2,1,0:T(8,128)(2,1)} %sink_ref.1, bf16[3,2,32,256]{3,2,1,0:T(8,128)(2,1)} %src_ref.1, s32[1,96]{1,0:T(1,128)} %bitcast.5), custom_call_target="tpu_custom_call" | custom-call | flops 7000000000 | bytes 4000000 | tf_op jit(solution)/shard_map/pallas_call | solution.py:382
  44.6 1.3 %copy.6 = f32[1,2,12,96]{3,1,2,0:T(2,128)} copy(f32[1,2,12,96]{3,1,2,0:T(2,128)} %bitcast.4) | data formatting | bytes 18432

commit v4 on v3

--- a/solution.py
+++ b/solution.py
@@ -43,9 +43,32 @@
     def dev(x_, y_, z_, c_):
         return ((z_ % 4) * 8 + x_ * 2 + c_, y_ * 2 + z_ // 4)
 
+    xs4 = [x] + [lax.rem(x + d, 4) for d in range(1, 4)]
+    ys4 = [y] + [lax.rem(y + d, 4) for d in range(1, 4)]
+    first_tm = tm // 8 * 8
+    z_hi = op % 2
+
+    def near(x_, y_, c_):
+        return (first_tm + x_ * 2 + c_, y_ * 2 + z_hi)
+
     def block_of(x_, y_):
-        p = (x_ + 4 - y_) % 4
-        return y_ % 2 + 2 * (p // 2), p % 2
+        p = lax.rem(x_ + 4 - y_, 4)
+        r = lax.rem(p, 2)
+        return lax.rem(y_, 2) + p - r, r
+
+    my_ys, my_r = block_of(x, y)
+    other_core = near(x, y, 1 - core)
+    sends = {}
+    owners = {}
+    for cls in range(1, 8):
+        for lh in range(2):
+            dx, dy = HOPS[cls][lh]
+            sends[cls, lh] = near(xs4[dx], ys4[dy], lh), block_of(xs4[dx], ys4[dy])
+        (dx0, dy0), (dx1, dy1) = HOPS[cls]
+        x0, y0, x1, y1 = xs4[-dx0 % 4], ys4[-dy0 % 4], xs4[-dx1 % 4], ys4[-dy1 % 4]
+        xo, yo = x0 + core * (x1 - x0), y0 + core * (y1 - y0)
+        for cs in range(2):
+            owners[cls, cs] = near(xo, yo, cs)
 
     cp_src = pltpu.make_async_copy(src_ref, src_v, in_sem.at[0])
     cp_per = pltpu.make_async_copy(peram_ref.at[0], per_v, in_sem.at[1])
@@ -62,22 +85,22 @@
 
     barrier = pltpu.get_barrier_semaphore()
 
-    @pl.loop(1, 32)
-    def _(k):
-        pl.semaphore_signal(
-            barrier, inc=1,
-            device_id=dev((x + k // 2) % 4, (y + k // 8) % 4, z, (core + k) % 2),
-            device_id_type=MESH,
-        )
+    for y_n in ys4:
+        for x_n in xs4:
+            for c_n in (1 - core, core):
+                if not (x_n is x and y_n is y and c_n is core):
+                    pl.semaphore_signal(barrier, inc=1, device_id=near(x_n, y_n, c_n), device_id_type=MESH)
 
     z_up = (z + 1) % 8
     z_dn = (z + 7) % 8
+    above = dev(x, y, z_up, core)
+    below = dev(x, y, z_dn, core)
     later_up = z < 7
     later_dn = z == 0
     for z_n, later in ((z_up, later_up), (z_dn, later_dn)):
         @pl.when(later)
         def _():
-            pl.semaphore_signal(barrier, inc=1, device_id=dev(x, y, z_n, core), device_id_type=MESH)
+            pl.semaphore_signal(barrier, inc=1, device_id=above if z_n is z_up else below, device_id_type=MESH)
 
     def turned(g):
         cp_sink[g].wait()
@@ -104,21 +127,21 @@
     for z_n, later, at in ((z_up, later_up, 1), (z_dn, later_dn, 0)):
         @pl.when(jnp.logical_not(later))
         def _():
-            pl.semaphore_signal(answer.at[at], inc=1, device_id=dev(x, y, z_n, core), device_id_type=MESH)
+            pl.semaphore_signal(answer.at[at], inc=1, device_id=above if z_n is z_up else below, device_id_type=MESH)
 
     first = []
     for r in range(2):
         for far in range(2):
-            xd = (2 * (y // 2) + r + y + 2 * far) % 4
-            yd = (y + 2 * far) % 4
+            xd = lax.rem(2 * y - lax.rem(y, 2) + r + 2 * far, 4)
+            yd = ys4[2 * far]
             for lh in range(2):
                 src = src_v.at[:, :, pl.ds(16 * r, 16), pl.ds(128 * lh, 128)]
-                me8 = ((x + 4 - xd) % 4) * 2 + core
+                me8 = lax.rem(x + 4 - xd, 4) * 2 + core
                 dst = sring.at[0, me8]
                 k = (r * 2 + far) * 2 + lh
                 cp = pltpu.make_async_remote_copy(
                     src, dst, s1_send.at[k], s1_recv.at[me8],
-                    device_id=dev(xd, yd, z, lh), device_id_type=MESH,
+                    device_id=near(xd, yd, lh), device_id_type=MESH,
                 )
                 if far:
                     cp.start()
@@ -141,7 +164,7 @@
             sring.at[slot_from, pl.ds(2 * ch, 2)], sring.at[slot_to, pl.ds(2 * ch, 2)],
             ring_send.at[slot_from, ch] if z_n is z_up else ring_send.at[8 + slot_from, ch],
             ring_recv.at[slot_to, ch],
-            device_id=dev(x, y, z_n, core), device_id_type=MESH,
+            device_id=above if z_n is z_up else below, device_id_type=MESH,
         )
 
     ring_cps = []
@@ -195,7 +218,6 @@
                         fs[h, zl, pl.ds(xs * 6 + c * 24 + cs * 3 + j, 16, STRIDE_S), :] = tile
 
     t_cps = []
-    my_ys, my_r = block_of(x, y)
 
     def send_turned(g):
         for cls in (0, 1, 2, 3, 4, 7, 5, 6):
@@ -203,20 +225,18 @@
                 cp = pltpu.make_async_remote_copy(
                     tout.at[my_ys, my_r, 1 - core, g], recv.at[core, g],
                     t_send.at[g, 0], t_recv.at[core, g],
-                    device_id=dev(x, y, z, 1 - core), device_id_type=MESH,
+                    device_id=other_core, device_id_type=MESH,
                 )
                 cp.start()
                 t_cps.append(cp)
                 pltpu.make_async_copy(tout.at[my_ys, my_r, core, g], recv.at[core, g], t_recv.at[core, g]).start()
                 continue
             for lh in range(2):
-                dx, dy = HOPS[cls][lh]
-                xd, yd = (x + dx) % 4, (y + dy) % 4
-                ys, r = block_of(xd, yd)
+                target, (ys, r) = sends[cls, lh]
                 cp = pltpu.make_async_remote_copy(
                     tout.at[ys, r, lh, g], recv.at[2 * cls + core, g],
                     t_send.at[g, 2 * cls + lh], t_recv.at[2 * cls + core, g],
-                    device_id=dev(xd, yd, z, lh), device_id_type=MESH,
+                    device_id=target, device_id_type=MESH,
                 )
                 cp.start()
                 t_cps.append(cp)
@@ -334,20 +354,16 @@
         if cls == 0:
             cp = pltpu.make_async_remote_copy(
                 oret.at[:, 1 - core], ogot.at[:, core], o_send.at[0], o_recv.at[core],
-                device_id=dev(x, y, z, 1 - core), device_id_type=MESH,
+                device_id=other_core, device_id_type=MESH,
             )
             cp.start()
             o_cps.append(cp)
             continue
-        (dx0, dy0), (dx1, dy1) = HOPS[cls]
-        dx = dx0 + core * (dx1 - dx0)
-        dy = dy0 + core * (dy1 - dy0)
-        xd, yd = (x + 4 - dx) % 4, (y + 4 - dy) % 4
         for cs in range(2):
             cp = pltpu.make_async_remote_copy(
                 oret.at[:, 2 * cls + cs], ogot.at[:, 2 * cls + core],
                 o_send.at[2 * cls + cs], o_recv.at[2 * cls + core],
-                device_id=dev(xd, yd, z, cs), device_id_type=MESH,
+                device_id=owners[cls, cs], device_id_type=MESH,
             )
             cp.start()
             o_cps.append(cp)

time: 46 us -> 45.5 us (0.989)
  Pallas kernels: 44.6 us -> 44 us
    pallas_call x1, Pallas kernels: 44.6 us -> 44 us  [local(): pl.pallas_call(kernel, out_shape=jax.ShapeDtypeStruct((12, 2, 96), F32),...]
where the time goes in v4:
time: 45.5 us; the launch traced here: 45.3 us
  Pallas kernels  44 us (97%)
  local copies, waits for them, and re-layouts  1.31 us (3%)
    pallas_call x1, Pallas kernels, local(): pl.pallas_call(kernel, out_shape=jax.ShapeDtypeStruct((12, 2, 96), F32),...  44 us
    unnamed x1, local copies, waits for them, and re-layouts  1.31 us

profile of v4, /device:TPU:1, one launch (start us, length us, event | category | flops | bytes accessed | tf_op | source)
XLA Modules:
  0.0 45.3 jit_solution(5822544868722360430)
XLA Ops:
  0.0 44.0 %shard_map.46 = f32[12,2,96]{2,1,0:T(2,128)} custom-call(bf16[1,2,256,256]{3,2,1,0:T(8,128)(2,1)} %peram_ref.1, bf16[1,12,2,256,256]{4,3,2,1,0:T(8,128)(2,1)} %sink_ref.1, bf16[3,2,32,256]{3,2,1,0:T(8,128)(2,1)} %src_ref.1, s32[1,96]{1,0:T(1,128)} %bitcast.5), custom_call_target="tpu_custom_call" | custom-call | flops 7000000000 | bytes 4000000 | tf_op jit(solution)/shard_map/pallas_call | solution.py:398
  44.0 1.3 %copy.6 = f32[1,2,12,96]{3,1,2,0:T(2,128)} copy(f32[1,2,12,96]{3,1,2,0:T(2,128)} %bitcast.4) | data formatting | bytes 18432

commit v5 on v4

--- a/solution.py
+++ b/solution.py
@@ -309,6 +309,15 @@
         ring_step(3, ch)
     place_source(2)
     place_source(6)
+    cp_lab.wait()
+    labels = jnp.broadcast_to(lab_v[...].astype(F32), (8, 96))
+    lane = lax.broadcasted_iota(jnp.int32, (8, 96), 1)
+    sub = lax.broadcasted_iota(jnp.int32, (8, 96), 0) % 4
+    same = []
+    for g in range(GROUPS):
+        own = jnp.sum(jnp.where(lane == op * 12 + 4 * g + sub, labels, 0.0), axis=1, keepdims=True)
+        same.append((own == labels).astype(F32))
+
     gather_rows(0)
     for ch in range(4):
         ring_step(4, ch)
@@ -319,15 +328,6 @@
         for ch in range(4):
             ring_wait(slot, ch)
         place_source(slot)
-
-    cp_lab.wait()
-    labels = jnp.broadcast_to(lab_v[...].astype(F32), (8, 96))
-    lane = lax.broadcasted_iota(jnp.int32, (8, 96), 1)
-    sub = lax.broadcasted_iota(jnp.int32, (8, 96), 0) % 4
-    same = []
-    for g in range(GROUPS):
-        own = jnp.sum(jnp.where(lane == op * 12 + 4 * g + sub, labels, 0.0), axis=1, keepdims=True)
-        same.append((own == labels).astype(F32))
 
     o_cps = []
 

time: 45.5 us -> 45.4 us (level)
  no operation moved by 1% of the time
where the time goes in v5:
time: 45.4 us; the launch traced here: 45.2 us
  Pallas kernels  43.9 us (97%)
  local copies, waits for them, and re-layouts  1.31 us (3%)
    pallas_call x1, Pallas kernels, local(): pl.pallas_call(kernel, out_shape=jax.ShapeDtypeStruct((12, 2, 96), F32),...  43.9 us
    unnamed x1, local copies, waits for them, and re-layouts  1.31 us

profile of v5, /device:TPU:1, one launch (start us, length us, event | category | flops | bytes accessed | tf_op | source)
XLA Modules:
  0.0 45.2 jit_solution(9727369430256062558)
XLA Ops:
  0.0 43.9 %shard_map.46 = f32[12,2,96]{2,1,0:T(2,128)} custom-call(bf16[1,2,256,256]{3,2,1,0:T(8,128)(2,1)} %peram_ref.1, bf16[1,12,2,256,256]{4,3,2,1,0:T(8,128)(2,1)} %sink_ref.1, bf16[3,2,32,256]{3,2,1,0:T(8,128)(2,1)} %src_ref.1, s32[1,96]{1,0:T(1,128)} %bitcast.5), custom_call_target="tpu_custom_call" | custom-call | flops 7000000000 | bytes 4000000 | tf_op jit(solution)/shard_map/pallas_call | solution.py:398
  43.9 1.3 %copy.6 = f32[1,2,12,96]{3,1,2,0:T(2,128)} copy(f32[1,2,12,96]{3,1,2,0:T(2,128)} %bitcast.4) | data formatting | bytes 18432
